TPU v7x, 32 devices: a whole 2x2x4 slice. The times are simulated.
32 devices in a mesh: groups: 2 (over x), dp: 16 (over z, y, core).
Axes of the slice: x: 2, y: 2, z: 4, core: 2. Of those that a mesh axis runs over, the one named last changes fastest.
Arguments:
- layer_inputs: bfloat16 [128, 64, 4096], P(('groups', 'dp')), parts along dimension 0, may hold values from -6 to 6
- out_grads: bfloat16 [128, 64, 14336], P(('groups', 'dp')), parts along dimension 0, may hold values from -6 to 6
- lengths: int32 [128], P(('groups', 'dp')), parts along dimension 0, may hold values from 1 to 64
- p_in: bfloat16 [32, 4096], replicated, may hold values from -0.09375 to 0.09375
- p_out: bfloat16 [64, 14336], replicated, may hold values from -0.046875 to 0.046875
- test_proj: bfloat16 [128, 2048], P(('groups', 'dp')), parts along dimension 0, may hold values from -6 to 6
Outputs:
- fisher: float32 [4096, 2048], P(('groups', 'dp')), parts along dimension 0
- scores: float32 [128, 64], P(('groups', 'dp')), parts along dimension 0
There are 2 independent parts, one for each index of `groups`. A program takes and returns all parts, laid end to end along the dimension named above; an argument that names none is the same for every part. Nothing has to cross between parts.
All inputs are finite; a program needn't handle non-finite values.
Results may differ from a plain program's by a relative error of at most 0.015.
Values may be sent and summed in bfloat16 or wider, within the bound.
A program may use at most 128 MiB of HBM per device.

v0:
```python
import jax
import jax.numpy as jnp
from jax import lax
from jax.sharding import PartitionSpec as P


def local(layer_inputs, out_grads, lengths, p_in, p_out, test_proj):
    seq_count, seq_len, model_width = layer_inputs.shape
    hidden_width = out_grads.shape[2]
    live_mask = (jnp.arange(seq_len)[None, :] < lengths[:, None]).astype(jnp.float32)
    left_proj = jnp.dot(
        layer_inputs.reshape(seq_count * seq_len, model_width),
        p_in.T,
        preferred_element_type=jnp.float32,
    ).reshape(seq_count, seq_len, p_in.shape[0])
    right_proj = jnp.dot(
        out_grads.reshape(seq_count * seq_len, hidden_width),
        p_out.T,
        preferred_element_type=jnp.float32,
    ).reshape(seq_count, seq_len, p_out.shape[0])
    right_proj = right_proj * live_mask[:, :, None]
    features = p_in.shape[0] * p_out.shape[0]
    proj = (
        jnp.einsum("slo,sli->soi", right_proj, left_proj)
        .reshape(seq_count, features)
        .astype(jnp.bfloat16)
    )
    row_count = features // lax.axis_size("dp")
    first_row = lax.axis_index("dp") * row_count
    proj_wide = proj.astype(jnp.float32)
    gram_rows = lax.psum_scatter(
        jnp.dot(proj.T, proj, preferred_element_type=jnp.float32),
        "dp",
        scatter_dimension=0,
        tiled=True,
    )
    block = lax.dynamic_slice_in_dim(gram_rows, first_row, row_count, 1)
    trace = lax.psum(jnp.trace(block), "dp")
    fisher = gram_rows * (features / trace)
    rms_train = jnp.sqrt(jnp.mean(proj_wide * proj_wide, axis=1) + 1e-06)
    root_features = jnp.sqrt(jnp.float32(features))
    piece = lax.all_gather(test_proj, "dp", axis=0, tiled=True)
    piece_wide = piece.astype(jnp.float32)
    rms_test = jnp.sqrt(jnp.mean(piece_wide * piece_wide, axis=1) + 1e-06)
    inner = jnp.dot(proj, piece.T, preferred_element_type=jnp.float32)
    scores = inner / (rms_train[:, None] * rms_test[None, :] * root_features)
    return (fisher, scores)


def solution(mesh):
    return jax.shard_map(
        local,
        mesh=mesh,
        in_specs=(
            P(("groups", "dp"), None, None),
            P(("groups", "dp"), None, None),
            P(("groups", "dp")),
            P(),
            P(),
            P(("groups", "dp"), None),
        ),
        out_specs=(P(("groups", "dp"), None), P(("groups", "dp"), None)),
        check_vma=False,
    )
```

profile of v0, /device:TPU:0, one launch (start us, length us, event | category | flops | bytes accessed | tf_op | source)
XLA Modules:
  0.0 249.4 jit_solution(9823727572313118086)
XLA Ops:
  7.2 0.0 copy-start
  7.2 0.0 reduce-scatter.2.cloned.1.call-start
  7.2 0.9 fusion.16
  8.1 0.7 copy-done
  8.8 6.7 %multiply_reduce_fusion.1 = (f32[4]{0:T(128)S(1)}, bf16[4,64,32]{1,2,0:T(8,128)(2,1)S(1)}) fusion(bf16[4,64,4096]{2,1,0:T(8,128)(2,1)S(1)} %copy-done, bf16[32,4096]{1,0:T(8,128)(2,1)} %param.9, bf16[4,64,14336]{2,1,0:T(8,128)(2,1)} %param.7, bf16[64,14336]{1,0:T(8,128)(2,1)} %param.10, f32[4,64]{1,0:T(4,128)S(1)} %fusion.16), kind=kOutput, calls=%fused_computation.10 | convolution fusion | flops 537968640 | bytes 11551760 | tf_op jit(solution)/shard_map/slo,sli->soi/dot_general | solution.py:24
  15.5 0.1 copy.9
  15.6 0.1 convert_element_type.25
  15.7 8.1 %fusion.21 = f32[2048,2048]{1,0:T(8,128)} fusion(bf16[4,2048]{1,0:T(4,128)(2,1)S(1)} %convert_element_type.25), kind=kOutput, calls=%fused_computation.18 | convolution fusion | flops 33554432 | bytes 16793600 | tf_op jit(solution)/shard_map/dot_general | solution.py:32
  23.8 0.0 copy-start.1
  23.8 0.0 reduce-scatter.2.cloned.1.call-update
  23.8 0.7 copy-done.1
  24.5 23.8 %all-gather = bf16[16,4,2048]{2,1,0:T(4,128)(2,1)S(1)} all-gather(bf16[1,4,2048]{2,1,0:T(4,128)(2,1)S(1)} %bitcast.24), channel_id=1, replica_groups=mesh['groups'=2,'dp'=16] {'dp'}, dimensions={0}, use_global_device_ids=true | all-gather | bytes 278528 | tf_op jit(solution)/shard_map/all_gather | solution.py:42
  48.3 0.1 reshape.49
  48.4 0.2 multiply_reduce_fusion
  48.6 156.7 %reduce-scatter.2.cloned.1.call-done = f32[128,2048]{1,0:T(8,128)} async-done(((f32[2048,2048]{1,0:T(8,128)}), f32[128,2048]{1,0:T(8,128)}) %reduce-scatter.2.cloned.1.call-update) | async-done | bytes 1048592 | tf_op jit(solution)/shard_map/reduce_scatter | solution.py:31
  205.3 1.5 select_reduce_fusion
  206.7 0.8 convolution_divide_fusion
  207.5 32.1 %psum.7 = f32[]{:T(128)} all-reduce(f32[]{:T(128)} %select_reduce_fusion), channel_id=1, replica_groups=mesh['groups'=2,'dp'=16] {'dp'}, use_global_device_ids=true, to_apply=%region_2.3 | all-reduce | flops 1 | bytes 8 | tf_op jit(solution)/shard_map/psum | solution.py:38
  240.3 2.3 broadcast_multiply_fusion
  (2 shorter events, 0.0 us)
Async XLA Ops:
  7.2 1.6 copy-start
  7.2 198.1 %reduce-scatter.2.cloned.1.call-start = ((), (), s32[]{:S(2)}) async-start(), calls=%async_computation.1 | async-start | bytes 17825792 | tf_op jit(solution)/shard_map/reduce_scatter | solution.py:31
  23.8 0.7 copy-start.1
Sparse Core Ops, SparseCore 0:
  24.0 181.2 reduce-scatter.1
where the time goes:
time: 250 us; the launch traced here: 249 us
  waiting for transfers between devices  157 us (63%)
  blocking collectives  55.9 us (22%)
  matrix products  15.6 us (6%)
  between operations  14.8 us (6%)
  other arithmetic  4.79 us (2%)
    reduce_scatter x1, waiting for transfers between devices, local(): lax.psum_scatter(jnp.dot(proj.T, proj, preferred_element_type=jnp.float32...  157 us
    psum x1, blocking collectives, local(): trace = lax.psum(jnp.trace(block), 'dp')  32.1 us
    all_gather x1, blocking collectives, local(): piece = lax.all_gather(test_proj, 'dp', axis=0, tiled=True)  23.8 us
    dot_general x1, matrix products, local(): jnp.dot(proj.T, proj, preferred_element_type=jnp.float32)  8.1 us
    dot_general x1, matrix products, local(): jnp.einsum('slo,sli->soi', right_proj, left_proj)  6.7 us
  transfers between devices with their start and end apart: 1, of which 1 were waited for; matrix products, arithmetic and copies ran while one was open for 0% of the time, Pallas kernels for 0%

commit v1 on v0

--- a/solution.py
+++ b/solution.py
@@ -7,6 +7,7 @@
 def local(layer_inputs, out_grads, lengths, p_in, p_out, test_proj):
     seq_count, seq_len, model_width = layer_inputs.shape
     hidden_width = out_grads.shape[2]
+    test_all = lax.all_gather(test_proj, "dp", axis=0, tiled=True)
     live_mask = (jnp.arange(seq_len)[None, :] < lengths[:, None]).astype(jnp.float32)
     left_proj = jnp.dot(
         layer_inputs.reshape(seq_count * seq_len, model_width),
@@ -27,22 +28,18 @@
     )
     row_count = features // lax.axis_size("dp")
     first_row = lax.axis_index("dp") * row_count
+    proj_all = lax.all_gather(proj, "dp", axis=0, tiled=True)
+    mine = lax.dynamic_slice_in_dim(proj_all, first_row, row_count, 1)
+    gram_rows = jnp.dot(mine.T, proj_all, preferred_element_type=jnp.float32)
+    all_wide = proj_all.astype(jnp.float32)
+    trace = jnp.sum(all_wide * all_wide)
+    fisher = gram_rows * (features / trace)
     proj_wide = proj.astype(jnp.float32)
-    gram_rows = lax.psum_scatter(
-        jnp.dot(proj.T, proj, preferred_element_type=jnp.float32),
-        "dp",
-        scatter_dimension=0,
-        tiled=True,
-    )
-    block = lax.dynamic_slice_in_dim(gram_rows, first_row, row_count, 1)
-    trace = lax.psum(jnp.trace(block), "dp")
-    fisher = gram_rows * (features / trace)
     rms_train = jnp.sqrt(jnp.mean(proj_wide * proj_wide, axis=1) + 1e-06)
     root_features = jnp.sqrt(jnp.float32(features))
-    piece = lax.all_gather(test_proj, "dp", axis=0, tiled=True)
-    piece_wide = piece.astype(jnp.float32)
-    rms_test = jnp.sqrt(jnp.mean(piece_wide * piece_wide, axis=1) + 1e-06)
-    inner = jnp.dot(proj, piece.T, preferred_element_type=jnp.float32)
+    test_wide = test_all.astype(jnp.float32)
+    rms_test = jnp.sqrt(jnp.mean(test_wide * test_wide, axis=1) + 1e-06)
+    inner = jnp.dot(proj, test_all.T, preferred_element_type=jnp.float32)
     scores = inner / (rms_train[:, None] * rms_test[None, :] * root_features)
     return (fisher, scores)
 

time: 250 us -> 55.3 us (0.22)
  waiting for transfers between devices: 157 us -> 0 us
  blocking collectives: 55.9 us -> 42 us
  between operations: 14.8 us -> 1.37 us
  matrix products: 15.6 us -> 8.77 us
  other arithmetic: 4.79 us -> 1.78 us
    reduce_scatter x1 -> x0, waiting for transfers between devices: 157 us -> none  [local(): lax.psum_scatter(jnp.dot(proj.T, proj, preferred_element_type=jnp.float32...]
    psum x1 -> x0, blocking collectives: 32.1 us -> none  [local(): trace = lax.psum(jnp.trace(block), 'dp')]
    all_gather x1 -> x2, blocking collectives: 23.8 us -> 42 us  [the longest x1 23.8 us: local(): proj_all = lax.all_gather(proj, 'dp', axis=0, tiled=True)]
    dot_general x2, matrix products: 8.86 us -> 2.06 us  [the longest x1 1.29 us: local(): gram_rows = jnp.dot(mine.T, proj_all, preferred_element_type=jnp.float32)]
  transfers between devices with their start and end apart: 1 -> 0, of which waited for: 1 -> 0; matrix products, arithmetic and copies ran while one was open for 0% -> 0% of each run, Pallas kernels for 0% -> 0%
where the time goes in v1:
time: 55.3 us; the launch traced here: 55.1 us
  blocking collectives  42 us (76%)
  matrix products  8.77 us (16%)
  other arithmetic  1.78 us (3%)
  between operations  1.37 us (2%)
  local copies, waits for them, and re-layouts  1.22 us (2%)
    all_gather x1, blocking collectives, local(): proj_all = lax.all_gather(proj, 'dp', axis=0, tiled=True)  23.8 us
    all_gather x1, blocking collectives, local(): test_all = lax.all_gather(test_proj, 'dp', axis=0, tiled=True)  18.2 us
    dot_general x1, matrix products, local(): jnp.einsum('slo,sli->soi', right_proj, left_proj)  6.71 us
    dot_general x1, matrix products, local(): gram_rows = jnp.dot(mine.T, proj_all, preferred_element_type=jnp.float32)  1.29 us

profile of v1, /device:TPU:0, one launch (start us, length us, event | category | flops | bytes accessed | tf_op | source)
XLA Modules:
  0.0 55.1 jit_solution(7487127783041173244)
XLA Ops:
  0.6 0.0 copy-start
  0.6 0.9 %fusion.17 = f32[4,64]{1,0:T(4,128)S(1)} fusion(s32[4]{0:T(128)} %param.8), kind=kLoop, calls=%fused_computation.15 | loop fusion | flops 512 | bytes 1040 | tf_op jit(solution)/shard_map/convert_element_type | solution.py:11
  1.5 0.7 %copy-done = bf16[4,64,4096]{2,1,0:T(8,128)(2,1)S(1)} copy-done((bf16[4,64,4096]{2,1,0:T(8,128)(2,1)S(1)}, bf16[4,64,4096]{2,1,0:T(8,128)(2,1)}, u32[]{:S(2)}) %copy-start) | copy-done | bytes 2097176
  2.2 0.0 copy-start.1
  2.2 6.7 %multiply_reduce_fusion.2 = (f32[4]{0:T(128)S(1)}, bf16[4,64,32]{1,2,0:T(8,128)(2,1)S(1)}) fusion(bf16[4,64,4096]{2,1,0:T(8,128)(2,1)S(1)} %copy-done, bf16[32,4096]{1,0:T(8,128)(2,1)} %param.9, bf16[4,64,14336]{2,1,0:T(8,128)(2,1)} %param.7, bf16[64,14336]{1,0:T(8,128)(2,1)} %param.10, f32[4,64]{1,0:T(4,128)S(1)} %fusion.17), kind=kOutput, calls=%fused_computation.11 | convolution fusion | flops 537968640 | bytes 11551760 | tf_op jit(solution)/shard_map/slo,sli->soi/dot_general | solution.py:25
  9.0 0.1 copy.10
  9.1 0.1 convert_element_type.26
  9.2 0.1 reshape.46
  9.3 23.8 %all-gather = bf16[16,4,2048]{2,1,0:T(4,128)(2,1)S(1)} all-gather(bf16[1,4,2048]{2,1,0:T(4,128)(2,1)S(1)} %reshape.46), channel_id=1, replica_groups=mesh['groups'=2,'dp'=16] {'dp'}, dimensions={0}, use_global_device_ids=true | all-gather | bytes 278528 | tf_op jit(solution)/shard_map/all_gather | solution.py:31
  33.1 0.1 reshape.47
  33.2 0.7 %multiply_reduce_fusion.1 = f32[]{:T(128)} fusion(bf16[64,2048]{1,0:T(8,128)(2,1)S(1)} %reshape.47), kind=kLoop, calls=%fused_computation.9 | loop fusion | flops 393215 | bytes 262148 | tf_op jit(solution)/shard_map/reduce_sum | solution.py:35
  34.6 0.0 copy-done.1
  34.6 18.2 %all-gather.1 = bf16[16,4,2048]{2,1,0:T(4,128)(2,1)S(1)} all-gather(bf16[1,4,2048]{2,1,0:T(4,128)(2,1)S(1)} %bitcast.23), channel_id=1, replica_groups=mesh['groups'=2,'dp'=16] {'dp'}, dimensions={0}, use_global_device_ids=true | all-gather | bytes 278528 | tf_op jit(solution)/shard_map/all_gather | solution.py:10
  52.8 0.1 reshape.49
  52.9 0.2 multiply_reduce_fusion
  53.0 0.8 %convolution_divide_fusion = f32[4,64]{1,0:T(4,128)} fusion(bf16[4,2048]{1,0:T(4,128)(2,1)S(1)} %convert_element_type.26, bf16[64,2048]{1,0:T(8,128)(2,1)S(1)} %reshape.49, f32[64]{0:T(128)S(1)} %add_sqrt_fusion, f32[4]{0:T(128)S(1)} %add_sqrt_fusion.1), kind=kOutput, calls=%fused_computation.6 | convolution fusion | flops 1049344 | bytes 279824 | tf_op jit(solution)/shard_map/dot_general | solution.py:42
  53.8 1.3 %convolution_multiply_fusion = f32[128,2048]{1,0:T(8,128)} fusion(bf16[64,2048]{1,0:T(8,128)(2,1)S(1)} %reshape.47, f32[]{:T(128)S(6)} %div.15, s32[]{:T(128)S(6)} %select_n.3), kind=kOutput, calls=%fused_computation | convolution fusion | flops 33816576 | bytes 1327112 | tf_op jit(solution)/shard_map/dot_general | solution.py:33
  (2 shorter events, 0.0 us)
Async XLA Ops:
  0.6 1.6 %copy-start = (bf16[4,64,4096]{2,1,0:T(8,128)(2,1)S(1)}, bf16[4,64,4096]{2,1,0:T(8,128)(2,1)}, u32[]{:S(2)}) copy-start(bf16[4,64,4096]{2,1,0:T(8,128)(2,1)} %param.6) | copy-start | bytes 6291460
  2.2 32.4 %copy-start.1 = (bf16[4,2048]{1,0:T(4,128)(2,1)S(1)}, bf16[4,2048]{1,0:T(4,128)(2,1)}, u32[]{:S(2)}) copy-start(bf16[4,2048]{1,0:T(4,128)(2,1)} %param.11) | copy-start | bytes 49156

commit v2 on v1

v2 whole, which is shorter than its diff:
```python
import functools

import jax
import jax.numpy as jnp
from jax import lax
from jax.experimental import pallas as pl
from jax.experimental.pallas import tpu as pltpu
from jax.sharding import PartitionSpec as P

LANES = 128
HALVES = 2
MESH = pl.DeviceIdType.MESH


def chunk_count(width):
    for count in (7, 4, 2, 1):
        if width % (count * LANES) == 0:
            return count
    return 1


def dot_last(a, b):
    return lax.dot_general(a, b, (((1,), (1,)), ((), ())), preferred_element_type=jnp.float32)


def dot_first(a, b):
    return lax.dot_general(a, b, (((0,), (0,)), ((), ())), preferred_element_type=jnp.float32)


def hi_lo(a):
    hi = a.astype(jnp.bfloat16)
    return hi, (a - hi.astype(jnp.float32)).astype(jnp.bfloat16)


def kernel(
    n, k_in, k_out,
    len_ref, x_hbm, g_hbm, pin_hbm, pout_hbm, test_ref,
    fisher_ref, scores_ref,
    x_v, g_v, pin_v, pout_v,
    gath0, gath1, gtest,
    wide, wide_test, blocks, test_rows, fold, own, own_test, gram_tmp,
    sem_x, sem_g, sem_pin, sem_pout,
    send_a, send_b, recv,
):
    seqs, seq_len, _ = x_hbm.shape
    per = seqs // HALVES
    group_rows = LANES // k_in
    features = k_in * k_out
    nb = features // LANES
    chips = n // 2
    chunks = g_v.shape[1]
    width = g_v.shape[4]
    all_seqs = n * seqs

    me = lax.axis_index("dp")
    groups_me = lax.axis_index("groups")
    core = lax.rem(me, 2)
    chip = me // 2
    mate = chip * 2 + 1 - core

    def peer(k):
        return lax.rem(chip + k, chips) * 2 + core

    def x_copy(h):
        return pltpu.make_async_copy(x_hbm.at[pl.ds(h * per, per)], x_v.at[h], sem_x.at[h])

    def g_copy(h, c):
        start = pl.multiple_of(c * width, LANES)
        return pltpu.make_async_copy(
            g_hbm.at[pl.ds(h * per, per), :, pl.ds(start, width)], g_v.at[h, c], sem_g.at[h, c]
        )

    def pout_copy(c):
        start = pl.multiple_of(c * width, LANES)
        return pltpu.make_async_copy(pout_hbm.at[:, pl.ds(start, width)], pout_v.at[c], sem_pout.at[c])

    pin_copy = pltpu.make_async_copy(pin_hbm, pin_v, sem_pin)

    pin_copy.start()
    x_copy(0).start()

    @pl.loop(0, chunks)
    def _(c):
        pout_copy(c).start()
        g_copy(0, c).start()

    x_copy(1).start()

    @pl.loop(0, chunks)
    def _(c):
        g_copy(1, c).start()

    barrier = pltpu.get_barrier_semaphore()
    pl.semaphore_signal(barrier, inc=1, device_id=(groups_me, mate), device_id_type=MESH)

    @pl.loop(1, chips)
    def _(k):
        pl.semaphore_signal(barrier, inc=1, device_id=(groups_me, peer(k)), device_id_type=MESH)

    test_wide = test_ref[...].astype(jnp.float32)
    for b in range(nb):
        own_test[pl.ds(b, seqs, stride=nb), :] = test_wide[:, b * LANES:(b + 1) * LANES]
    gtest[me] = own_test[...].astype(jnp.bfloat16)

    pl.semaphore_wait(barrier, chips)

    def own_send(kind, buf, k):
        return pltpu.make_async_remote_copy(
            src_ref=buf.at[me], dst_ref=buf.at[me],
            send_sem=send_a.at[kind, k], recv_sem=recv.at[kind, me],
            device_id=(groups_me, peer(k)), device_id_type=MESH,
        )

    def forward(kind, buf, src, k):
        return pltpu.make_async_remote_copy(
            src_ref=buf.at[src], dst_ref=buf.at[src],
            send_sem=send_b.at[kind, k], recv_sem=recv.at[kind, src],
            device_id=(groups_me, mate), device_id_type=MESH,
        )

    def arrived(kind, buf, src):
        return pltpu.make_async_remote_copy(
            src_ref=buf.at[src], dst_ref=buf.at[src],
            send_sem=send_b.at[kind, 0], recv_sem=recv.at[kind, src],
            device_id=(groups_me, mate), device_id_type=MESH,
        )

    def send_own(kind, buf):
        @pl.loop(1, chips)
        def _(k):
            own_send(kind, buf, k).start()

        forward(kind, buf, me, 0).start()

    def pass_on(kind, buf):
        @pl.loop(1, chips)
        def _(k):
            src = peer(k)
            arrived(kind, buf, src).wait_recv()
            forward(kind, buf, src, k).start()

    def rest(kind, buf):
        @pl.loop(0, chips)
        def _(k):
            src = lax.rem(chip + k, chips) * 2 + 1 - core
            arrived(kind, buf, src).wait_recv()

    def drain(kind, buf):
        forward(kind, buf, me, 0).wait_send()

        @pl.loop(1, chips)
        def _(k):
            own_send(kind, buf, k).wait_send()
            forward(kind, buf, peer(k), k).wait_send()

    send_own(0, gtest)

    lane = lax.broadcasted_iota(jnp.int32, (nb, LANES), 1) // k_in
    token = lax.broadcasted_iota(jnp.int32, (seq_len, k_out), 0)

    pin_copy.wait()

    def right_part(h, low, high, total, first):
        def step(c, total):
            if first:
                pout_copy(c).wait()
            g_copy(h, c).wait()
            return total + dot_last(g_v[h, c].reshape(per * seq_len, width), pout_v[c])
        return lax.fori_loop(low, high, step, total)

    def finish(h, left, right, buf):
        for q in range(per):
            s = h * per + q
            rows = slice(q * seq_len, (q + 1) * seq_len)
            live = jnp.where(token < len_ref[s], right[rows], 0.0)
            rh, rl = hi_lo(live)
            lh, ll = hi_lo(left[rows])
            prod = dot_first(
                jnp.concatenate([rh, rh, rl], axis=0), jnp.concatenate([lh, ll, lh], axis=0)
            )
            fold[q] = prod
            tile = fold[q, pl.ds(0, nb, stride=group_rows), :]
            for k in range(1, group_rows):
                tile = jnp.where(lane == k, fold[q, pl.ds(k, nb, stride=group_rows), :], tile)
            tile = tile.astype(jnp.bfloat16)
            buf[me, q * nb:(q + 1) * nb, :] = tile
            own[s * nb:(s + 1) * nb, :] = tile.astype(jnp.float32)

    def left_part(h):
        x_copy(h).wait()
        pin = jnp.concatenate([pin_v[...]] * group_rows, axis=0)
        return dot_last(x_v[h].reshape(per * seq_len, x_v.shape[3]), pin)

    zero = jnp.zeros((per * seq_len, k_out), jnp.float32)
    mid = (chunks + 1) // 2

    left = left_part(0)
    right = right_part(0, 0, chunks, zero, True)
    finish(0, left, right, gath0)
    send_own(1, gath0)
    pass_on(0, gtest)

    left = left_part(1)
    right = right_part(1, 0, mid, zero, False)
    pass_on(1, gath0)
    right = right_part(1, mid, chunks, right, False)
    finish(1, left, right, gath1)
    send_own(2, gath1)

    rest(0, gtest)
    wide_test[...] = gtest[...].reshape(wide_test.shape).astype(jnp.float32)
    squares = jnp.zeros((all_seqs, LANES), jnp.float32)
    for b in range(nb):
        rows = wide_test[pl.ds(b, all_seqs, stride=nb), :]
        squares += rows * rows
        test_rows[:, b * LANES:(b + 1) * LANES] = rows.astype(jnp.bfloat16)
    own_rows = [own[pl.ds(b, seqs, stride=nb), :] for b in range(nb)]
    own_squares = own_rows[0] * own_rows[0]
    for b in range(1, nb):
        own_squares += own_rows[b] * own_rows[b]
    mean_train = jnp.sum(own_squares, axis=1, keepdims=True) / features
    mean_test = lax.dot_general(
        jnp.ones((seqs, LANES), jnp.float32), squares, (((1,), (1,)), ((), ())),
        precision=lax.Precision.HIGHEST, preferred_element_type=jnp.float32,
    ) / features
    inner = dot_last(jnp.concatenate(own_rows, axis=1).astype(jnp.bfloat16), test_rows[...])
    scores_ref[...] = inner / (
        jnp.sqrt(mean_train + 1e-06) * jnp.sqrt(mean_test + 1e-06) * jnp.sqrt(jnp.float32(features))
    )

    rest(1, gath0)
    half_rows = n * per * nb
    half_seqs = n * per

    def spread(h, buf):
        wide[pl.ds(h * half_rows, half_rows), :] = buf[...].reshape(half_rows, LANES).astype(jnp.float32)
        total = jnp.zeros((half_seqs, LANES), jnp.float32)
        for b in range(nb):
            rows = wide[pl.ds(h * half_rows + b, half_seqs, stride=nb), :]
            total += rows * rows
            blocks[b, h * half_seqs:(h + 1) * half_seqs, :] = rows.astype(jnp.bfloat16)
        return total

    total = spread(0, gath0)
    pass_on(2, gath1)
    rest(2, gath1)
    total += spread(1, gath1)
    scale = features / jnp.sum(total)

    row_count = fisher_ref.shape[0]
    first_row = me * row_count
    if row_count % LANES == 0:
        for r in range(row_count // LANES):
            mine = blocks[first_row // LANES + r]
            for b in range(nb):
                fisher_ref[r * LANES:(r + 1) * LANES, b * LANES:(b + 1) * LANES] = (
                    dot_first(mine, blocks[b]) * scale
                )
    else:
        mine = blocks[first_row // LANES]
        offset = pl.multiple_of(lax.rem(first_row, LANES), row_count)
        for b in range(nb):
            gram_tmp[...] = dot_first(mine, blocks[b]) * scale
            fisher_ref[:, b * LANES:(b + 1) * LANES] = gram_tmp[pl.ds(offset, row_count), :]

    drain(0, gtest)
    drain(1, gath0)
    drain(2, gath1)


def local(layer_inputs, out_grads, lengths, p_in, p_out, test_proj):
    n = lax.axis_size("dp")
    seqs, seq_len, model_width = layer_inputs.shape
    hidden = out_grads.shape[2]
    k_in, k_out = p_in.shape[0], p_out.shape[0]
    features = k_in * k_out
    nb = features // LANES
    chunks = chunk_count(hidden)
    width = hidden // chunks
    per = seqs // HALVES
    chips = n // 2
    f32, bf16 = jnp.float32, jnp.bfloat16
    dma = pltpu.SemaphoreType.DMA
    anywhere = pl.BlockSpec(memory_space=pl.ANY)
    vmem = pl.BlockSpec(memory_space=pltpu.VMEM)
    return pl.pallas_call(
        functools.partial(kernel, n, k_in, k_out),
        out_shape=(
            jax.ShapeDtypeStruct((features // n, features), f32),
            jax.ShapeDtypeStruct((seqs, n * seqs), f32),
        ),
        in_specs=[pl.BlockSpec(memory_space=pltpu.SMEM)] + [anywhere] * 4 + [vmem],
        out_specs=(vmem, vmem),
        scratch_shapes=[
            pltpu.VMEM((HALVES, per, seq_len, model_width), bf16),
            pltpu.VMEM((HALVES, chunks, per, seq_len, width), bf16),
            pltpu.VMEM((k_in, model_width), bf16),
            pltpu.VMEM((chunks, k_out, width), bf16),
            pltpu.VMEM((n, per * nb, LANES), bf16),
            pltpu.VMEM((n, per * nb, LANES), bf16),
            pltpu.VMEM((n, seqs * nb, LANES), bf16),
            pltpu.VMEM((n * seqs * nb, LANES), f32),
            pltpu.VMEM((n * seqs * nb, LANES), f32),
            pltpu.VMEM((nb, n * seqs, LANES), bf16),
            pltpu.VMEM((n * seqs, features), bf16),
            pltpu.VMEM((per, k_out, LANES), f32),
            pltpu.VMEM((seqs * nb, LANES), f32),
            pltpu.VMEM((seqs * nb, LANES), f32),
            pltpu.VMEM((LANES, LANES), f32),
            dma((HALVES,)),
            dma((HALVES, chunks)),
            dma,
            dma((chunks,)),
            dma((3, chips)),
            dma((3, chips)),
            dma((3, n)),
        ],
        compiler_params=pltpu.CompilerParams(
            collective_id=0, has_side_effects=True, vmem_limit_bytes=48 * 1024 * 1024
        ),
        cost_estimate=pl.CostEstimate(
            flops=2 * seqs * seq_len * (hidden * k_out + model_width * k_in),
            bytes_accessed=2 * (seqs * seq_len + k_out) * hidden,
            transcendentals=0,
        ),
    )(lengths, layer_inputs, out_grads, p_in, p_out, test_proj)


def solution(mesh):
    return jax.shard_map(
        local,
        mesh=mesh,
        in_specs=(
            P(("groups", "dp"), None, None),
            P(("groups", "dp"), None, None),
            P(("groups", "dp")),
            P(),
            P(),
            P(("groups", "dp"), None),
        ),
        out_specs=(P(("groups", "dp"), None), P(("groups", "dp"), None)),
        check_vma=False,
    )
```

time: 55.3 us -> 29.5 us (0.53)
  the two profiles are of different devices: /device:TPU:0 before, /device:TPU:1 now
where the time goes in v2:
time: 29.5 us; the launch traced here: 29.2 us
  Pallas kernels  21.6 us (73%)
  local copies, waits for them, and re-layouts  6.95 us (24%)
  between operations  0.65 us (2%)
    pallas_call x1, Pallas kernels, local(): pl.pallas_call(functools.partial(kernel, n, k_in, k_out), out_shape=(jax....  21.6 us
    unnamed x12, local copies, waits for them, and re-layouts  6.95 us

profile of v2, /device:TPU:1, one launch (start us, length us, event | category | flops | bytes accessed | tf_op | source)
XLA Modules:
  0.0 29.2 jit_solution(12512588119302820339)
XLA Ops:
  0.6 0.0 copy-start
  0.6 1.6 %copy-done = bf16[4,64,4096]{2,1,0:T(8,128)(2,1)S(1)} copy-done((bf16[4,64,4096]{2,1,0:T(8,128)(2,1)S(1)}, bf16[4,64,4096]{2,1,0:T(8,128)(2,1)}, u32[]{:S(2)}) %copy-start) | copy-done | bytes 2097176
  2.2 0.0 copy-start.1
  2.2 1.5 %copy-done.1 = bf16[64,14336]{1,0:T(8,128)(2,1)S(1)} copy-done((bf16[64,14336]{1,0:T(8,128)(2,1)S(1)}, bf16[64,14336]{1,0:T(8,128)(2,1)}, u32[]{:S(2)}) %copy-start.1) | copy-done | bytes 1835032
  3.7 0.0 copy-start.2
  3.7 0.9 %copy-done.2 = bf16[32,4096]{1,0:T(8,128)(2,1)S(1)} copy-done((bf16[32,4096]{1,0:T(8,128)(2,1)S(1)}, bf16[32,4096]{1,0:T(8,128)(2,1)}, u32[]{:S(2)}) %copy-start.2) | copy-done | bytes 262168
  4.7 0.0 copy-start.3
  4.7 0.7 %copy-done.3 = bf16[4,2048]{1,0:T(4,128)(2,1)S(1)} copy-done((bf16[4,2048]{1,0:T(4,128)(2,1)S(1)}, bf16[4,2048]{1,0:T(4,128)(2,1)}, u32[]{:S(2)}) %copy-start.3) | copy-done | bytes 16408
  5.4 0.0 copy-start.4
  5.4 0.7 %copy-done.4 = s32[4]{0:T(128)S(1)} copy-done((s32[4]{0:T(128)S(1)}, s32[4]{0:T(128)}, u32[]{:S(2)}) %copy-start.4) | copy-done | bytes 40
  6.0 21.6 %shard_map.77 = (f32[128,2048]{1,0:T(8,128)S(1)}, f32[4,64]{1,0:T(4,128)S(1)}) custom-call(s32[4]{0:T(128)S(1)} %copy-done.4, bf16[4,64,4096]{2,1,0:T(8,128)(2,1)S(1)} %copy-done, bf16[4,64,14336]{2,1,0:T(8,128)(2,1)} %g_hbm.1, bf16[32,4096]{1,0:T(8,128)(2,1)S(1)} %copy-done.2, bf16[64,14336]{1,0:T(8,128)(2,1)S(1)} %copy-done.1, bf16[4,2048]{1,0:T(4,128)(2,1)S(1)} %copy-done.3), custom_call_target="tpu_custom_call" | custom-call | flops 536870912 | bytes 9175040 | tf_op jit(solution)/shard_map/pallas_call | solution.py:286
  27.7 1.0 %copy.10 = f32[128,2048]{1,0:T(8,128)} copy(f32[128,2048]{1,0:T(8,128)S(1)} %get-tuple-element.4) | data formatting | bytes 2097152
  28.6 0.6 %copy.11 = f32[4,64]{1,0:T(4,128)} copy(f32[4,64]{1,0:T(4,128)S(1)} %get-tuple-element.5) | data formatting | bytes 2048
Async XLA Ops:
  0.6 1.6 %copy-start = (bf16[4,64,4096]{2,1,0:T(8,128)(2,1)S(1)}, bf16[4,64,4096]{2,1,0:T(8,128)(2,1)}, u32[]{:S(2)}) copy-start(bf16[4,64,4096]{2,1,0:T(8,128)(2,1)} %x_hbm.1) | copy-start | bytes 6291460
  2.2 1.5 %copy-start.1 = (bf16[64,14336]{1,0:T(8,128)(2,1)S(1)}, bf16[64,14336]{1,0:T(8,128)(2,1)}, u32[]{:S(2)}) copy-start(bf16[64,14336]{1,0:T(8,128)(2,1)} %pout_hbm.1) | copy-start | bytes 5505028
  3.7 0.9 %copy-start.2 = (bf16[32,4096]{1,0:T(8,128)(2,1)S(1)}, bf16[32,4096]{1,0:T(8,128)(2,1)}, u32[]{:S(2)}) copy-start(bf16[32,4096]{1,0:T(8,128)(2,1)} %pin_hbm.1) | copy-start | bytes 786436
  4.7 0.7 %copy-start.3 = (bf16[4,2048]{1,0:T(4,128)(2,1)S(1)}, bf16[4,2048]{1,0:T(4,128)(2,1)}, u32[]{:S(2)}) copy-start(bf16[4,2048]{1,0:T(4,128)(2,1)} %test_ref.1) | copy-start | bytes 49156
  5.4 0.7 %copy-start.4 = (s32[4]{0:T(128)S(1)}, s32[4]{0:T(128)}, u32[]{:S(2)}) copy-start(s32[4]{0:T(128)} %len_ref.1) | copy-start | bytes 52

commit v3 on v2

--- a/solution.py
+++ b/solution.py
@@ -34,32 +34,27 @@
 
 def kernel(
     n, k_in, k_out,
-    len_ref, x_hbm, g_hbm, pin_hbm, pout_hbm, test_ref,
+    len_ref, x_hbm, g_hbm, pin_hbm, pout_hbm, test_hbm,
     fisher_ref, scores_ref,
-    x_v, g_v, pin_v, pout_v,
+    x_v, g_v, pin_v, pout_v, test_v,
     gath0, gath1, gtest,
     wide, wide_test, blocks, test_rows, fold, own, own_test, gram_tmp,
-    sem_x, sem_g, sem_pin, sem_pout,
-    send_a, send_b, recv,
+    sem_x, sem_g, sem_pin, sem_pout, sem_test,
+    send, recv,
 ):
     seqs, seq_len, _ = x_hbm.shape
     per = seqs // HALVES
     group_rows = LANES // k_in
     features = k_in * k_out
     nb = features // LANES
-    chips = n // 2
     chunks = g_v.shape[1]
     width = g_v.shape[4]
     all_seqs = n * seqs
 
     me = lax.axis_index("dp")
     groups_me = lax.axis_index("groups")
-    core = lax.rem(me, 2)
-    chip = me // 2
-    mate = chip * 2 + 1 - core
-
     def peer(k):
-        return lax.rem(chip + k, chips) * 2 + core
+        return lax.rem(me + k, n)
 
     def x_copy(h):
         return pltpu.make_async_copy(x_hbm.at[pl.ds(h * per, per)], x_v.at[h], sem_x.at[h])
@@ -76,6 +71,9 @@
 
     pin_copy = pltpu.make_async_copy(pin_hbm, pin_v, sem_pin)
 
+    test_copy = pltpu.make_async_copy(test_hbm, test_v, sem_test)
+
+    test_copy.start()
     pin_copy.start()
     x_copy(0).start()
 
@@ -91,67 +89,48 @@
         g_copy(1, c).start()
 
     barrier = pltpu.get_barrier_semaphore()
-    pl.semaphore_signal(barrier, inc=1, device_id=(groups_me, mate), device_id_type=MESH)
-
-    @pl.loop(1, chips)
+
+    @pl.loop(1, n)
     def _(k):
         pl.semaphore_signal(barrier, inc=1, device_id=(groups_me, peer(k)), device_id_type=MESH)
 
-    test_wide = test_ref[...].astype(jnp.float32)
+    test_copy.wait()
+    test_wide = test_v[...].astype(jnp.float32)
     for b in range(nb):
         own_test[pl.ds(b, seqs, stride=nb), :] = test_wide[:, b * LANES:(b + 1) * LANES]
     gtest[me] = own_test[...].astype(jnp.bfloat16)
 
-    pl.semaphore_wait(barrier, chips)
-
-    def own_send(kind, buf, k):
+    pl.semaphore_wait(barrier, n - 1)
+
+    def push(kind, buf, k):
         return pltpu.make_async_remote_copy(
             src_ref=buf.at[me], dst_ref=buf.at[me],
-            send_sem=send_a.at[kind, k], recv_sem=recv.at[kind, me],
+            send_sem=send.at[kind, k], recv_sem=recv.at[kind, me],
             device_id=(groups_me, peer(k)), device_id_type=MESH,
         )
 
-    def forward(kind, buf, src, k):
+    def pull(kind, buf, k):
+        src = peer(k)
         return pltpu.make_async_remote_copy(
             src_ref=buf.at[src], dst_ref=buf.at[src],
-            send_sem=send_b.at[kind, k], recv_sem=recv.at[kind, src],
-            device_id=(groups_me, mate), device_id_type=MESH,
+            send_sem=send.at[kind, k], recv_sem=recv.at[kind, src],
+            device_id=(groups_me, src), device_id_type=MESH,
         )
 
-    def arrived(kind, buf, src):
-        return pltpu.make_async_remote_copy(
-            src_ref=buf.at[src], dst_ref=buf.at[src],
-            send_sem=send_b.at[kind, 0], recv_sem=recv.at[kind, src],
-            device_id=(groups_me, mate), device_id_type=MESH,
-        )
-
     def send_own(kind, buf):
-        @pl.loop(1, chips)
+        @pl.loop(1, n)
         def _(k):
-            own_send(kind, buf, k).start()
-
-        forward(kind, buf, me, 0).start()
-
-    def pass_on(kind, buf):
-        @pl.loop(1, chips)
+            push(kind, buf, k).start()
+
+    def rest(kind, buf):
+        @pl.loop(1, n)
         def _(k):
-            src = peer(k)
-            arrived(kind, buf, src).wait_recv()
-            forward(kind, buf, src, k).start()
-
-    def rest(kind, buf):
-        @pl.loop(0, chips)
+            pull(kind, buf, k).wait_recv()
+
+    def drain(kind, buf):
+        @pl.loop(1, n)
         def _(k):
-            src = lax.rem(chip + k, chips) * 2 + 1 - core
-            arrived(kind, buf, src).wait_recv()
-
-    def drain(kind, buf):
-        forward(kind, buf, me, 0).wait_send()
-
-        @pl.loop(1, chips)
-        def _(k):
-            own_send(kind, buf, k).wait_send()
-            forward(kind, buf, peer(k), k).wait_send()
+            push(kind, buf, k).wait_send()
 
     send_own(0, gtest)
 
@@ -198,11 +177,9 @@
     right = right_part(0, 0, chunks, zero, True)
     finish(0, left, right, gath0)
     send_own(1, gath0)
-    pass_on(0, gtest)
 
     left = left_part(1)
     right = right_part(1, 0, mid, zero, False)
-    pass_on(1, gath0)
     right = right_part(1, mid, chunks, right, False)
     finish(1, left, right, gath1)
     send_own(2, gath1)
@@ -242,7 +219,6 @@
         return total
 
     total = spread(0, gath0)
-    pass_on(2, gath1)
     rest(2, gath1)
     total += spread(1, gath1)
     scale = features / jnp.sum(total)
@@ -278,10 +254,9 @@
     chunks = chunk_count(hidden)
     width = hidden // chunks
     per = seqs // HALVES
-    chips = n // 2
     f32, bf16 = jnp.float32, jnp.bfloat16
     dma = pltpu.SemaphoreType.DMA
-    anywhere = pl.BlockSpec(memory_space=pl.ANY)
+    anywhere = pl.BlockSpec(memory_space=pltpu.HBM)
     vmem = pl.BlockSpec(memory_space=pltpu.VMEM)
     return pl.pallas_call(
         functools.partial(kernel, n, k_in, k_out),
@@ -289,13 +264,14 @@
             jax.ShapeDtypeStruct((features // n, features), f32),
             jax.ShapeDtypeStruct((seqs, n * seqs), f32),
         ),
-        in_specs=[pl.BlockSpec(memory_space=pltpu.SMEM)] + [anywhere] * 4 + [vmem],
+        in_specs=[pl.BlockSpec(memory_space=pltpu.SMEM)] + [anywhere] * 5,
         out_specs=(vmem, vmem),
         scratch_shapes=[
             pltpu.VMEM((HALVES, per, seq_len, model_width), bf16),
             pltpu.VMEM((HALVES, chunks, per, seq_len, width), bf16),
             pltpu.VMEM((k_in, model_width), bf16),
             pltpu.VMEM((chunks, k_out, width), bf16),
+            pltpu.VMEM((seqs, features), bf16),
             pltpu.VMEM((n, per * nb, LANES), bf16),
             pltpu.VMEM((n, per * nb, LANES), bf16),
             pltpu.VMEM((n, seqs * nb, LANES), bf16),
@@ -311,12 +287,12 @@
             dma((HALVES, chunks)),
             dma,
             dma((chunks,)),
-            dma((3, chips)),
-            dma((3, chips)),
+            dma,
+            dma((3, n)),
             dma((3, n)),
         ],
         compiler_params=pltpu.CompilerParams(
-            collective_id=0, has_side_effects=True, vmem_limit_bytes=48 * 1024 * 1024
+            collective_id=0, has_side_effects=True, vmem_limit_bytes=57 * 1024 * 1024
         ),
         cost_estimate=pl.CostEstimate(
             flops=2 * seqs * seq_len * (hidden * k_out + model_width * k_in),

time: 29.5 us -> 25.4 us (0.86)
  the two profiles are of different devices: /device:TPU:1 before, /device:TPU:0 now
where the time goes in v3:
time: 25.4 us; the launch traced here: 25.1 us
  Pallas kernels  21.6 us (85%)
  local copies, waits for them, and re-layouts  2.88 us (11%)
  between operations  0.65 us (3%)
    pallas_call x1, Pallas kernels, local(): pl.pallas_call(functools.partial(kernel, n, k_in, k_out), out_shape=(jax....  21.6 us
    unnamed x4, local copies, waits for them, and re-layouts  2.88 us

profile of v3, /device:TPU:0, one launch (start us, length us, event | category | flops | bytes accessed | tf_op | source)
XLA Modules:
  0.0 25.1 jit_solution(624812643786533627)
XLA Ops:
  0.6 21.6 %shard_map.77 = (f32[128,2048]{1,0:T(8,128)}, f32[4,64]{1,0:T(4,128)}) custom-call(s32[4]{0:T(128)} %len_ref.1, bf16[4,64,4096]{2,1,0:T(8,128)(2,1)} %x_hbm.1, bf16[4,64,14336]{2,1,0:T(8,128)(2,1)} %g_hbm.1, bf16[32,4096]{1,0:T(8,128)(2,1)} %pin_hbm.1, bf16[64,14336]{1,0:T(8,128)(2,1)} %pout_hbm.1, bf16[4,2048]{1,0:T(4,128)(2,1)} %test_hbm.1), custom_call_target="tpu_custom_call" | custom-call | flops 536870912 | bytes 9175040 | tf_op jit(solution)/shard_map/pallas_call | solution.py:261
  22.2 0.0 copy-start
  22.3 2.3 %copy.10 = f32[128,2048]{1,0:T(8,128)} copy(f32[128,2048]{1,0:T(8,128)} %get-tuple-element.4) | data formatting | bytes 2097152
  24.5 0.0 copy-done
  24.6 0.6 %copy.11 = f32[4,64]{1,0:T(4,128)} copy(f32[4,64]{1,0:T(4,128)S(1)} %copy-done) | data formatting | bytes 2048
Async XLA Ops:
  22.2 2.3 %copy-start = (f32[4,64]{1,0:T(4,128)S(1)}, f32[4,64]{1,0:T(4,128)}, u32[]{:S(2)}) copy-start(f32[4,64]{1,0:T(4,128)} %get-tuple-element.5) | copy-start | bytes 3076

commit v4 on v3

--- a/solution.py
+++ b/solution.py
@@ -35,10 +35,10 @@
 def kernel(
     n, k_in, k_out,
     len_ref, x_hbm, g_hbm, pin_hbm, pout_hbm, test_hbm,
-    fisher_ref, scores_ref,
+    blocks, scale_ref, scores_ref,
     x_v, g_v, pin_v, pout_v, test_v,
     gath0, gath1, gtest,
-    wide, wide_test, blocks, test_rows, fold, own, own_test, gram_tmp,
+    wide, wide_test, test_rows, fold, own, own_test,
     sem_x, sem_g, sem_pin, sem_pout, sem_test,
     send, recv,
 ):
@@ -223,6 +223,18 @@
     total += spread(1, gath1)
     scale = features / jnp.sum(total)
 
+    scale_ref[...] = jnp.full(scale_ref.shape, scale, jnp.float32)
+
+    drain(0, gtest)
+    drain(1, gath0)
+    drain(2, gath1)
+
+
+def gram_kernel(blocks, scale_ref, scores_in, fisher_ref, scores_ref, gram_tmp):
+    me = lax.axis_index("dp")
+    nb = blocks.shape[0]
+    scale = scale_ref[0:1, :]
+    scores_ref[...] = scores_in[...]
     row_count = fisher_ref.shape[0]
     first_row = me * row_count
     if row_count % LANES == 0:
@@ -239,10 +251,6 @@
             gram_tmp[...] = dot_first(mine, blocks[b]) * scale
             fisher_ref[:, b * LANES:(b + 1) * LANES] = gram_tmp[pl.ds(offset, row_count), :]
 
-    drain(0, gtest)
-    drain(1, gath0)
-    drain(2, gath1)
-
 
 def local(layer_inputs, out_grads, lengths, p_in, p_out, test_proj):
     n = lax.axis_size("dp")
@@ -258,14 +266,15 @@
     dma = pltpu.SemaphoreType.DMA
     anywhere = pl.BlockSpec(memory_space=pltpu.HBM)
     vmem = pl.BlockSpec(memory_space=pltpu.VMEM)
-    return pl.pallas_call(
+    blocks, scale, scores = pl.pallas_call(
         functools.partial(kernel, n, k_in, k_out),
         out_shape=(
-            jax.ShapeDtypeStruct((features // n, features), f32),
+            jax.ShapeDtypeStruct((nb, n * seqs, LANES), bf16),
+            jax.ShapeDtypeStruct((8, LANES), f32),
             jax.ShapeDtypeStruct((seqs, n * seqs), f32),
         ),
         in_specs=[pl.BlockSpec(memory_space=pltpu.SMEM)] + [anywhere] * 5,
-        out_specs=(vmem, vmem),
+        out_specs=(vmem, vmem, vmem),
         scratch_shapes=[
             pltpu.VMEM((HALVES, per, seq_len, model_width), bf16),
             pltpu.VMEM((HALVES, chunks, per, seq_len, width), bf16),
@@ -277,12 +286,10 @@
             pltpu.VMEM((n, seqs * nb, LANES), bf16),
             pltpu.VMEM((n * seqs * nb, LANES), f32),
             pltpu.VMEM((n * seqs * nb, LANES), f32),
-            pltpu.VMEM((nb, n * seqs, LANES), bf16),
             pltpu.VMEM((n * seqs, features), bf16),
             pltpu.VMEM((per, k_out, LANES), f32),
             pltpu.VMEM((seqs * nb, LANES), f32),
             pltpu.VMEM((seqs * nb, LANES), f32),
-            pltpu.VMEM((LANES, LANES), f32),
             dma((HALVES,)),
             dma((HALVES, chunks)),
             dma,
@@ -300,6 +307,17 @@
             transcendentals=0,
         ),
     )(lengths, layer_inputs, out_grads, p_in, p_out, test_proj)
+    return pl.pallas_call(
+        gram_kernel,
+        out_shape=(
+            jax.ShapeDtypeStruct((features // n, features), f32),
+            jax.ShapeDtypeStruct(scores.shape, f32),
+        ),
+        in_specs=[vmem, vmem, vmem],
+        out_specs=(vmem, vmem),
+        scratch_shapes=[pltpu.VMEM((LANES, LANES), f32)],
+        compiler_params=pltpu.CompilerParams(vmem_limit_bytes=57 * 1024 * 1024),
+    )(blocks, scale, scores)
 
 
 def solution(mesh):

time: 25.4 us -> 24.3 us (0.957)
  local copies, waits for them, and re-layouts: 2.88 us -> 0 us
  Pallas kernels: 21.6 us -> 23.4 us
    unnamed x4 -> x0, local copies, waits for them, and re-layouts: 2.88 us -> none
    pallas_call x0 -> x1, Pallas kernels: none -> 2.26 us  [local(): pl.pallas_call(gram_kernel, out_shape=(jax.ShapeDtypeStruct((features //...]
    pallas_call x1, Pallas kernels: 21.6 us -> 21.1 us  [local(): pl.pallas_call(functools.partial(kernel, n, k_in, k_out), out_shape=(jax....]
where the time goes in v4:
time: 24.3 us; the launch traced here: 24 us
  Pallas kernels  23.4 us (96%)
  between operations  0.64 us (3%)
    pallas_call x1, Pallas kernels, local(): pl.pallas_call(functools.partial(kernel, n, k_in, k_out), out_shape=(jax....  21.1 us
    pallas_call x1, Pallas kernels, local(): pl.pallas_call(gram_kernel, out_shape=(jax.ShapeDtypeStruct((features //...  2.26 us

profile of v4, /device:TPU:0, one launch (start us, length us, event | category | flops | bytes accessed | tf_op | source)
XLA Modules:
  0.0 24.0 jit_solution(102960696671473097)
XLA Ops:
  0.6 21.1 %shard_map.77 = (bf16[16,64,128]{2,1,0:T(8,128)(2,1)}, f32[8,128]{1,0:T(8,128)}, f32[4,64]{1,0:T(4,128)}) custom-call(s32[4]{0:T(128)} %len_ref.1, bf16[4,64,4096]{2,1,0:T(8,128)(2,1)} %x_hbm.1, bf16[4,64,14336]{2,1,0:T(8,128)(2,1)} %g_hbm.1, bf16[32,4096]{1,0:T(8,128)(2,1)} %pin_hbm.1, bf16[64,14336]{1,0:T(8,128)(2,1)} %pout_hbm.1, bf16[4,2048]{1,0:T(4,128)(2,1)} %test_hbm.1), custom_call_target="tpu_custom_call" | custom-call | flops 536870912 | bytes 9175040 | tf_op jit(solution)/shard_map/pallas_call | solution.py:269
  21.8 2.3 %shard_map.78 = (f32[128,2048]{1,0:T(8,128)}, f32[4,64]{1,0:T(4,128)}) custom-call(bf16[16,64,128]{2,1,0:T(8,128)(2,1)} %get-tuple-element.5.blocks, f32[8,128]{1,0:T(8,128)} %get-tuple-element.6.scale_ref, f32[4,64]{1,0:T(4,128)} %get-tuple-element.7.scores_in), custom_call_target="tpu_custom_call" | custom-call | tf_op jit(solution)/shard_map/pallas_call | solution.py:310

commit v5 on v4

--- a/solution.py
+++ b/solution.py
@@ -73,6 +73,12 @@
 
     test_copy = pltpu.make_async_copy(test_hbm, test_v, sem_test)
 
+    barrier = pltpu.get_barrier_semaphore()
+
+    @pl.loop(1, n)
+    def _(k):
+        pl.semaphore_signal(barrier, inc=1, device_id=(groups_me, peer(k)), device_id_type=MESH)
+
     test_copy.start()
     pin_copy.start()
     x_copy(0).start()
@@ -87,12 +93,6 @@
     @pl.loop(0, chunks)
     def _(c):
         g_copy(1, c).start()
-
-    barrier = pltpu.get_barrier_semaphore()
-
-    @pl.loop(1, n)
-    def _(k):
-        pl.semaphore_signal(barrier, inc=1, device_id=(groups_me, peer(k)), device_id_type=MESH)
 
     test_copy.wait()
     test_wide = test_v[...].astype(jnp.float32)

time: 24.3 us -> 24.2 us (level)
  no operation moved by 1% of the time
where the time goes in v5:
time: 24.2 us; the launch traced here: 23.9 us
  Pallas kernels  23.3 us (96%)
  between operations  0.64 us (3%)
    pallas_call x1, Pallas kernels, local(): pl.pallas_call(functools.partial(kernel, n, k_in, k_out), out_shape=(jax....  21 us
    pallas_call x1, Pallas kernels, local(): pl.pallas_call(gram_kernel, out_shape=(jax.ShapeDtypeStruct((features //...  2.27 us

profile of v5, /device:TPU:0, one launch (start us, length us, event | category | flops | bytes accessed | tf_op | source)
XLA Modules:
  0.0 23.9 jit_solution(12427046872532515244)
XLA Ops:
  0.6 21.0 %shard_map.77 = (bf16[16,64,128]{2,1,0:T(8,128)(2,1)}, f32[8,128]{1,0:T(8,128)}, f32[4,64]{1,0:T(4,128)}) custom-call(s32[4]{0:T(128)} %len_ref.1, bf16[4,64,4096]{2,1,0:T(8,128)(2,1)} %x_hbm.1, bf16[4,64,14336]{2,1,0:T(8,128)(2,1)} %g_hbm.1, bf16[32,4096]{1,0:T(8,128)(2,1)} %pin_hbm.1, bf16[64,14336]{1,0:T(8,128)(2,1)} %pout_hbm.1, bf16[4,2048]{1,0:T(4,128)(2,1)} %test_hbm.1), custom_call_target="tpu_custom_call" | custom-call | flops 536870912 | bytes 9175040 | tf_op jit(solution)/shard_map/pallas_call | solution.py:269
  21.6 2.3 %shard_map.78 = (f32[128,2048]{1,0:T(8,128)}, f32[4,64]{1,0:T(4,128)}) custom-call(bf16[16,64,128]{2,1,0:T(8,128)(2,1)} %get-tuple-element.5.blocks, f32[8,128]{1,0:T(8,128)} %get-tuple-element.6.scale_ref, f32[4,64]{1,0:T(4,128)} %get-tuple-element.7.scores_in), custom_call_target="tpu_custom_call" | custom-call | tf_op jit(solution)/shard_map/pallas_call | solution.py:310
